TPU v7x, 32 devices: a whole 2x2x4 slice. The times are simulated.
32 devices in a mesh: req: 8 (over y, x, core), mlp: 4 (over z).
Axes of the slice: x: 2, y: 2, z: 4, core: 2. Of those that a mesh axis runs over, the one named last changes fastest.
Arguments:
- tokens: bfloat16 [2048, 2560], P('req'), may hold values from -125 to 125
- lengths: int32 [8, 4], P('req'), may hold values from 1 to 128, 256 in all within a row
- page_table: int32 [8, 16], P('req'), may hold values from 0 to 15, each once within a row
- attn_norm: float32 [2560], replicated, may hold values from 0.25 to 1.75
- qkv_weight: bfloat16 [2560, 8, 768], P(None, 'mlp'), may hold values from -0.125 to 0.125
- q_norm: float32 [128], replicated, may hold values from 0.25 to 1.75
- k_norm: float32 [128], replicated, may hold values from 0.25 to 1.75
- o_weight: bfloat16 [4096, 2560], P('mlp'), may hold values from -0.09375 to 0.09375
- mlp_norm: float32 [2560], replicated, may hold values from 0.25 to 1.75
- gate_up: bfloat16 [9728, 2, 2560], P(('req', 'mlp')), may hold values from -0.125 to 0.125
- down_weight: bfloat16 [9728, 2560], P(('req', 'mlp')), may hold values from -0.0625 to 0.0625
Outputs:
- layer_out: bfloat16 [2048, 2560], P(('req', 'mlp'))
- kv_cache: bfloat16 [2, 128, 16, 8, 128], P(None, 'req', None, 'mlp')
Inputs may be any that keep to these rules, and one draw needn't show every extreme that they name: `lengths`: each row sums to 256, and the longest prompt of every pack is exactly 128. `page_table`: each row is a permutation of 0 .. 15.
All inputs are finite; a program needn't handle non-finite values.
Results may differ from a plain program's by a relative error of at most 0.0049.
Values may be sent and summed in bfloat16 or wider, within the bound.
A program may use at most 128 MiB of HBM per device.

v0:
```python
import math

import jax
import jax.numpy as jnp
from jax import lax
from jax.sharding import PartitionSpec as P

rope_theta = 1000000.0
norm_eps = 1e-06


def from_partner(value, axis, bit):
    mask = 2**bit
    pairs = [(source, source ^ mask) for source in range(lax.axis_size(axis))]
    return lax.ppermute(value, axis, pairs)


def rms_scale(values, gain):
    mean_sq = jnp.mean(values * values, axis=-1, keepdims=True)
    return values * lax.rsqrt(mean_sq + norm_eps) * gain


def positions_of(lengths, slots):
    ends = jnp.cumsum(lengths)
    slot_ids = jnp.arange(slots, dtype=jnp.int32)
    passed = (ends[None, :] <= slot_ids[:, None]).astype(jnp.int32)
    segment = jnp.sum(passed, axis=1)
    start = jnp.sum(passed * lengths[None, :], axis=1)
    return (slot_ids, segment, slot_ids - start)


def rotate(values, position, head_dim):
    half = head_dim // 2
    freq = rope_theta ** (-(2.0 * jnp.arange(half, dtype=jnp.float32)) / head_dim)
    angle = position.astype(jnp.float32)[:, None] * freq[None, :]
    shape = (angle.shape[0],) + (1,) * (values.ndim - 2) + (half,)
    cosine = jnp.cos(angle).reshape(shape)
    sine = jnp.sin(angle).reshape(shape)
    first = values[..., :half]
    second = values[..., half:]
    return jnp.concatenate(
        [first * cosine - second * sine, second * cosine + first * sine], axis=-1
    )


def feed_forward(rows, unit_pairs, unit_down):
    gate = jnp.einsum("td,fd->tf", rows, unit_pairs[:, 0, :], preferred_element_type=jnp.float32)
    upper = jnp.einsum("td,fd->tf", rows, unit_pairs[:, 1, :], preferred_element_type=jnp.float32)
    act = (jax.nn.silu(gate) * upper).astype(jnp.bfloat16)
    return jnp.dot(act, unit_down, preferred_element_type=jnp.float32)


def per_device(
    tokens,
    lengths,
    page_table,
    attn_norm,
    qkv_weight,
    q_norm,
    k_norm,
    o_weight,
    mlp_norm,
    gate_up,
    down_weight,
):
    slots = tokens.shape[0]
    head_dim = q_norm.shape[0]
    local_kv = qkv_weight.shape[1]
    group_q = qkv_weight.shape[2] // head_dim - 2
    pages = page_table.shape[1]
    page_rows = slots // pages
    owned = slots // lax.axis_size("mlp")
    slot_ids, segment, position = positions_of(lengths[0], slots)
    normed = rms_scale(tokens.astype(jnp.float32), attn_norm).astype(jnp.bfloat16)
    qkv = jnp.einsum("sd,dkc->skc", normed, qkv_weight, preferred_element_type=jnp.float32)
    query = qkv[:, :, : group_q * head_dim].reshape(slots, local_kv, group_q, head_dim)
    key = qkv[:, :, group_q * head_dim : (group_q + 1) * head_dim]
    value = qkv[:, :, (group_q + 1) * head_dim :]
    query = rotate(rms_scale(query, q_norm), position, head_dim).astype(jnp.bfloat16)
    key = rotate(rms_scale(key, k_norm), position, head_dim).astype(jnp.bfloat16)
    value = value.astype(jnp.bfloat16)
    key_pages = key.reshape(pages, page_rows, local_kv, head_dim)
    value_pages = value.reshape(pages, page_rows, local_kv, head_dim)
    kv_cache = jnp.zeros((2, pages, page_rows, local_kv, head_dim), jnp.bfloat16)
    kv_cache = kv_cache.at[:, page_table[0]].set(jnp.stack([key_pages, value_pages]))
    scores = jnp.einsum(
        "skgd,tkd->kgst", query, key, preferred_element_type=jnp.float32
    ) / math.sqrt(head_dim)
    allowed = (segment[:, None] == segment[None, :]) & (slot_ids[None, :] <= slot_ids[:, None])
    weights = jnp.where(allowed, jnp.exp(scores), 0.0)
    probs = (weights / jnp.sum(weights, axis=-1, keepdims=True)).astype(jnp.bfloat16)
    context = jnp.einsum("kgst,tkd->skgd", probs, value, preferred_element_type=jnp.float32)
    context = context.astype(jnp.bfloat16).reshape(slots, local_kv * group_q * head_dim)
    attn_out = lax.psum_scatter(
        jnp.dot(context, o_weight, preferred_element_type=jnp.float32),
        "mlp",
        scatter_dimension=0,
        tiled=True,
    )
    mine = lax.dynamic_slice_in_dim(tokens, lax.axis_index("mlp") * owned, owned, 0).astype(
        jnp.float32
    )
    resid = mine + attn_out
    mlp_in = rms_scale(resid, mlp_norm).astype(jnp.bfloat16)
    req_bits = lax.axis_size("req").bit_length() - 1
    low_bits = 2
    req_index = lax.axis_index("req")
    pooled = lax.all_gather(mlp_in, "mlp", axis=0, tiled=True)
    for bit in range(low_bits):
        partner = from_partner(pooled, "req", bit)
        upper_side = req_index // 2**bit % 2 == 1
        lower_rows = jnp.where(upper_side, partner, pooled)
        upper_rows = jnp.where(upper_side, pooled, partner)
        pooled = jnp.concatenate([lower_rows, upper_rows], axis=0)
    units = jnp.concatenate([gate_up, down_weight[:, None, :]], axis=1)
    for bit in range(low_bits, req_bits):
        far_units = from_partner(units, "req", bit)
        units = jnp.concatenate([units, far_units], axis=0)
    partial_out = feed_forward(pooled, units[:, 0:2, :], units[:, 2, :])
    for bit in reversed(range(low_bits)):
        half_rows = partial_out.shape[0] // 2
        upper_side = req_index // 2**bit % 2 == 1
        lower_part = partial_out[:half_rows]
        upper_part = partial_out[half_rows:]
        kept = jnp.where(upper_side, upper_part, lower_part)
        sent = jnp.where(upper_side, lower_part, upper_part)
        partial_out = kept + from_partner(sent.astype(jnp.bfloat16), "req", bit).astype(sent.dtype)
    mlp_out = lax.psum_scatter(
        partial_out.astype(jnp.bfloat16), "mlp", scatter_dimension=0, tiled=True
    ).astype(jnp.float32)
    layer_out = (resid + mlp_out).astype(jnp.bfloat16)
    return (layer_out, kv_cache)


def solution(mesh):
    return jax.shard_map(
        per_device,
        mesh=mesh,
        in_specs=(
            P("req", None),
            P("req", None),
            P("req", None),
            P(),
            P(None, "mlp", None),
            P(),
            P(),
            P("mlp", None),
            P(),
            P(("req", "mlp"), None, None),
            P(("req", "mlp"), None),
        ),
        out_specs=(P(("req", "mlp"), None), P(None, "req", None, "mlp", None)),
        check_vma=False,
    )
```

profile of v0, /device:TPU:0, one launch (start us, length us, event | category | flops | bytes accessed | tf_op | source)
XLA Modules:
  0.0 334.4 jit_solution(913210761727777834)
XLA Ops:
  7.2 1.7 fusion.5
  8.9 5.9 %fusion = f32[256,2,768]{2,0,1:T(8,128)S(1)} fusion(bf16[2560,2,768]{2,1,0:T(2,128)(2,1)} %param.15, bf16[256,2560]{1,0:T(8,128)(2,1)} %param.11, f32[2560]{0:T(1024)} %param.14, f32[256]{0:T(256)S(1)} %add_rsqrt_fusion.2), kind=kOutput, calls=%fused_computation.2 | convolution fusion | flops 2015887360 | bytes 10759168 | tf_op jit(solution)/shard_map/sd,dkc->skc/dot_general | solution.py:75
  21.3 1.7 convolution_convert_fusion
  23.8 3.0 fusion.34
  26.9 54.9 %reduce-scatter.3.cloned.1.call-done = f32[64,2560]{1,0:T(8,128)} async-done(((f32[256,2560]{1,0:T(8,128)}), f32[64,2560]{1,0:T(8,128)}) %reduce-scatter.3.cloned.1.call-update) | async-done | bytes 655376 | tf_op jit(solution)/shard_map/reduce_scatter | solution.py:94
  83.1 1.9 multiply_convert_fusion.2
  85.3 2.3 copy.56
  87.7 2.6 pad_maximum_fusion.2
  91.8 25.9 %all-gather.2.cloned.1.call-done = bf16[256,2560]{1,0:T(8,128)(2,1)} async-done(((bf16[64,2560]{1,0:T(8,128)(2,1)}), bf16[256,2560]{1,0:T(8,128)(2,1)}) %all-gather.2.cloned.1.call-update) | async-done | bytes 1310736 | tf_op jit(solution)/shard_map/all_gather | solution.py:108
  117.6 3.4 %collective-permute-done = bf16[256,2560]{1,0:T(8,128)(2,1)} collective-permute-done((bf16[256,2560]{1,0:T(8,128)(2,1)}, bf16[256,2560]{1,0:T(8,128)(2,1)}, u32[]{:S(2)}, u32[]{:S(2)}) %collective-permute-start) | collective-permute-done | bytes 1310752 | tf_op jit(solution)/shard_map/ppermute | solution.py:15
  121.0 1.9 broadcast_select_fusion.3
  122.9 1.9 pad_maximum_fusion.5
  126.8 66.1 %collective-permute-done.2 = bf16[304,3,2560]{2,0,1:T(8,128)(2,1)} collective-permute-done((bf16[304,3,2560]{2,0,1:T(8,128)(2,1)}, bf16[304,3,2560]{2,0,1:T(8,128)(2,1)}, u32[]{:S(2)}, u32[]{:S(2)}) %collective-permute-start.2) | collective-permute-done | bytes 4669472 | tf_op jit(solution)/shard_map/ppermute | solution.py:15
  192.9 4.5 %pad_maximum_fusion = bf16[608,3,2560]{2,0,1:T(8,128)(2,1)S(1)} fusion(bf16[304,3,2560]{2,0,1:T(8,128)(2,1)} %collective-permute-done.2, bf16[304,1,2560]{2,0,1:T(8,128)(2,1)} %bitcast.64, bf16[304,2,2560]{2,0,1:T(8,128)(2,1)S(1)} %copy.56), kind=kLoop, calls=%fused_computation.1 | loop fusion | flops 28016640 | bytes 18677760 | tf_op jit(solution)/shard_map/concatenate | solution.py:118
  197.5 4.2 %broadcast_select_fusion.1 = (bf16[512,2560]{1,0:T(8,128)(2,1)S(1)}, bf16[512,2560]{1,0:T(8,128)(2,1)S(1)}) fusion(bf16[512,2560]{1,0:T(8,128)(2,1)} %collective-permute-done.1, pred[]{:T(512)S(6)} %eq.30, bf16[256,2560]{1,0:T(8,128)(2,1)S(1)} %copy-done.3, bf16[256,2560]{1,0:T(8,128)(2,1)S(1)} %copy-done.1), kind=kLoop, calls=%fused_computation.23 | loop fusion | flops 7864320 | bytes 10485761 | tf_op jit(solution)/shard_map/jit(_where)/select_n | solution.py:112
  203.1 4.9 %fusion.3 = f32[1024,608]{0,1:T(8,128)} fusion(bf16[512,2560]{1,0:T(8,128)(2,1)S(1)} %get-tuple-element.15, bf16[512,2560]{1,0:T(8,128)(2,1)S(1)} %get-tuple-element.14, bf16[608,3,2560]{2,0,1:T(8,128)(2,1)S(1)} %pad_maximum_fusion), kind=kOutput, calls=%fused_computation.9 | convolution fusion | flops 3198156800 | bytes 10846208 | tf_op jit(solution)/shard_map/td,fd->tf/dot_general | solution.py:47
  208.0 13.9 %fusion.4 = f32[1024,2560]{1,0:T(8,128)} fusion(bf16[608,3,2560]{2,0,1:T(8,128)(2,1)} %copy-done.4, f32[1024,608]{0,1:T(8,128)} %fusion.3, bf16[512,2560]{1,0:T(8,128)(2,1)} %copy-done.8, bf16[512,2560]{1,0:T(8,128)(2,1)S(1)} %get-tuple-element.14), kind=kOutput, calls=%fused_computation.13 | convolution fusion | flops 6389563392 | bytes 24444928 | tf_op jit(solution)/shard_map/dot_general | solution.py:50
  222.0 4.5 %select_convert_fusion = bf16[512,2560]{1,0:T(8,128)(2,1)S(1)} fusion(f32[1024,2560]{1,0:T(8,128)} %fusion.4, pred[]{:T(512)S(6)} %eq.30), kind=kLoop, calls=%fused_computation.6 | loop fusion | flops 1310720 | bytes 7864321 | tf_op jit(solution)/shard_map/convert_element_type | solution.py:127
  228.0 56.1 %collective-permute-done.3 = bf16[512,2560]{1,0:T(8,128)(2,1)S(1)} collective-permute-done((bf16[512,2560]{1,0:T(8,128)(2,1)S(1)}, bf16[512,2560]{1,0:T(8,128)(2,1)S(1)}, u32[]{:S(2)}, u32[]{:S(2)}) %collective-permute-start.3) | collective-permute-done | bytes 2621472 | tf_op jit(solution)/shard_map/ppermute | solution.py:15
  284.1 5.3 %convert_add_fusion = f32[512,2560]{1,0:T(8,128)S(1)} fusion(bf16[512,2560]{1,0:T(8,128)(2,1)S(1)} %collective-permute-done.3, f32[1024,2560]{1,0:T(8,128)} %fusion.4, pred[]{:T(512)S(6)} %eq.30), kind=kLoop, calls=%fused_computation.5 | loop fusion | flops 3932160 | bytes 18350080 | tf_op jit(solution)/shard_map/add | solution.py:127
  289.8 3.0 collective-permute-done.4
  292.8 1.7 add_convert_fusion
  298.0 28.1 %reduce-scatter.5.cloned.1.call-done = bf16[64,2560]{1,0:T(8,128)(2,1)} async-done(((bf16[256,2560]{1,0:T(8,128)(2,1)}), bf16[64,2560]{1,0:T(8,128)(2,1)}) %reduce-scatter.5.cloned.1.call-update) | async-done | bytes 327696 | tf_op jit(solution)/shard_map/reduce_scatter | solution.py:128
  326.0 1.9 add_convert_fusion.2
  (75 shorter events, 19.0 us)
Async XLA Ops:
  7.2 74.7 %reduce-scatter.3.cloned.1.call-start = ((), (), s32[]{:S(2)}) async-start(), calls=%async_computation.2 | async-start | bytes 3276800 | tf_op jit(solution)/shard_map/reduce_scatter | solution.py:94
  14.8 1.4 copy-start.13
  16.2 2.1 copy-start.11
  16.6 2.9 copy-start.12
  21.2 2.3 slice-start
  21.2 2.6 slice-start.1
  26.8 55.0 %copy-start.7 = (bf16[256,2560]{1,0:T(8,128)(2,1)S(1)}, bf16[256,2560]{1,0:T(8,128)(2,1)}, u32[]{:S(2)}) copy-start(bf16[256,2560]{1,0:T(8,128)(2,1)} %param.11) | copy-start | bytes 3932164
  26.8 56.3 %copy-start.10 = (f32[2560]{0:T(1024)S(1)}, f32[2560]{0:T(1024)}, u32[]{:S(2)}) copy-start(f32[2560]{0:T(1024)} %param.19) | copy-start | bytes 30724
  26.9 90.8 %all-gather.2.cloned.1.call-start = ((), (), s32[]{:S(2)}) async-start(), calls=%async_computation.3 | async-start | bytes 1638400 | tf_op jit(solution)/shard_map/all_gather | solution.py:108
  85.1 240.9 %reduce-scatter.5.cloned.1.call-start = ((), (), s32[]{:S(2)}) async-start(), calls=%async_computation.4 | async-start | bytes 1638400 | tf_op jit(solution)/shard_map/reduce_scatter | solution.py:128
  85.3 2.3 copy-start.5
  90.3 102.7 %collective-permute-start.2 = (bf16[304,3,2560]{2,0,1:T(8,128)(2,1)}, bf16[304,3,2560]{2,0,1:T(8,128)(2,1)}, u32[]{:S(2)}, u32[]{:S(2)}) collective-permute-start(bf16[304,3,2560]{2,0,1:T(8,128)(2,1)} %pad_maximum_fusion.2), channel_id=1, source_target_pairs={{0,16},{4,20},{8,24},{12,28},{16,0},{20,4},{24,8},{28,12},{1,17},{... | collective-permute-start | bytes 14008328 | tf_op jit(solution)/shard_map/ppermute | solution.py:15
  117.6 3.4 %collective-permute-start = (bf16[256,2560]{1,0:T(8,128)(2,1)}, bf16[256,2560]{1,0:T(8,128)(2,1)}, u32[]{:S(2)}, u32[]{:S(2)}) collective-permute-start(bf16[256,2560]{1,0:T(8,128)(2,1)} %all-gather.2.cloned.1.call-done), channel_id=1, source_target_pairs={{0,4},{4,0},{8,12},{12,8},{16,20},{20,16},{24,28},{28,24},{1,5},{5... | collective-permute-start | bytes 3932168 | tf_op jit(solution)/shard_map/ppermute | solution.py:15
  122.9 1.9 copy-start
  122.9 2.4 copy-start.2
  125.3 72.1 %collective-permute-start.1 = (bf16[512,2560]{1,0:T(8,128)(2,1)}, bf16[512,2560]{1,0:T(8,128)(2,1)}, u32[]{:S(2)}, u32[]{:S(2)}) collective-permute-start(bf16[512,2560]{1,0:T(8,128)(2,1)} %pad_maximum_fusion.5), channel_id=1, source_target_pairs={{0,8},{4,12},{8,0},{12,4},{16,24},{20,28},{24,16},{28,20},{1,9},{5... | collective-permute-start | bytes 7864328 | tf_op jit(solution)/shard_map/ppermute | solution.py:15
  126.8 70.6 %copy-start.1 = (bf16[256,2560]{1,0:T(8,128)(2,1)S(1)}, bf16[256,2560]{1,0:T(8,128)(2,1)}, u32[]{:S(2)}) copy-start(bf16[256,2560]{1,0:T(8,128)(2,1)} %copy-done) | copy-start | bytes 3932164
  126.8 70.6 %copy-start.3 = (bf16[256,2560]{1,0:T(8,128)(2,1)S(1)}, bf16[256,2560]{1,0:T(8,128)(2,1)}, u32[]{:S(2)}) copy-start(bf16[256,2560]{1,0:T(8,128)(2,1)} %copy-done.2) | copy-start | bytes 3932164
  197.4 4.2 %copy-start.4 = (bf16[608,3,2560]{2,0,1:T(8,128)(2,1)}, bf16[608,3,2560]{2,0,1:T(8,128)(2,1)S(1)}, u32[]{:S(2)}) copy-start(bf16[608,3,2560]{2,0,1:T(8,128)(2,1)S(1)} %pad_maximum_fusion) | copy-start | bytes 28016644
  201.7 1.5 copy-start.8
  226.5 57.6 %collective-permute-start.3 = (bf16[512,2560]{1,0:T(8,128)(2,1)S(1)}, bf16[512,2560]{1,0:T(8,128)(2,1)S(1)}, u32[]{:S(2)}, u32[]{:S(2)}) collective-permute-start(bf16[512,2560]{1,0:T(8,128)(2,1)S(1)} %select_convert_fusion), channel_id=1, source_target_pairs={{0,8},{4,12},{8,0},{12,4},{16,24},{20,28},{24,16},{28,20},{1,9},{5... | collective-permute-start | bytes 7864328 | tf_op jit(solution)/shard_map/ppermute | solution.py:15
  289.7 6.0 %copy-start.14 = (s32[1,16]{1,0:T(1,128)S(1)}, s32[1,16]{1,0:T(1,128)}, u32[]{:S(2)}) copy-start(s32[1,16]{1,0:T(1,128)} %param.13) | copy-start | bytes 196
  289.7 3.1 collective-permute-start.4
  294.5 31.5 %copy-start.6 = (f32[64,2560]{1,0:T(8,128)S(1)}, f32[64,2560]{1,0:T(8,128)}, u32[]{:S(2)}) copy-start(f32[64,2560]{1,0:T(8,128)} %reduce-scatter.3.cloned.1.call-done) | copy-start | bytes 1966084
  (1 other events, 1.1 us)
Sparse Core Ops, SparseCore 0:
  27.0 54.7 reduce-scatter.2
  85.2 32.3 all-gather.1
  294.7 31.3 reduce-scatter.4
where the time goes:
time: 335 us; the launch traced here: 334 us
  waiting for transfers between devices  238 us (71%)
  other arithmetic  37.4 us (11%)
  matrix products  30.4 us (9%)
  between operations  14.1 us (4%)
  local copies, waits for them, and re-layouts  10.2 us (3%)
  starting transfers between devices  4.84 us (1%)
    ppermute x5, waiting for transfers between devices, from_partner(): return lax.ppermute(value, axis, pairs)  129 us
    reduce_scatter x1, waiting for transfers between devices, per_device(): lax.psum_scatter(jnp.dot(context, o_weight, preferred_element_type=jnp.fl...  54.9 us
    reduce_scatter x1, waiting for transfers between devices, per_device(): lax.psum_scatter(partial_out.astype(jnp.bfloat16), 'mlp', scatter_dimensi...  28.1 us
    all_gather x1, waiting for transfers between devices, per_device(): pooled = lax.all_gather(mlp_in, 'mlp', axis=0, tiled=True)  25.9 us
    dot_general x1, matrix products, feed_forward(): return jnp.dot(act, unit_down, preferred_element_type=jnp.float32)  13.9 us
    unnamed x36, local copies, waits for them, and re-layouts  7.07 us
  transfers between devices with their start and end apart: 8, of which 7 were waited for; matrix products, arithmetic and copies ran while one was open for 5% of the time, Pallas kernels for 0%

commit v1 on v0

--- a/solution.py
+++ b/solution.py
@@ -3,10 +3,13 @@
 import jax
 import jax.numpy as jnp
 from jax import lax
+from jax.experimental import pallas as pl
+from jax.experimental.pallas import tpu as pltpu
 from jax.sharding import PartitionSpec as P
 
 rope_theta = 1000000.0
 norm_eps = 1e-06
+MESH = pl.DeviceIdType.MESH
 
 
 def from_partner(value, axis, bit):
@@ -43,11 +46,361 @@
     )
 
 
-def feed_forward(rows, unit_pairs, unit_down):
-    gate = jnp.einsum("td,fd->tf", rows, unit_pairs[:, 0, :], preferred_element_type=jnp.float32)
-    upper = jnp.einsum("td,fd->tf", rows, unit_pairs[:, 1, :], preferred_element_type=jnp.float32)
-    act = (jax.nn.silu(gate) * upper).astype(jnp.bfloat16)
-    return jnp.dot(act, unit_down, preferred_element_type=jnp.float32)
+def exchange_kernel(
+    partial_ref,
+    mine_ref,
+    norm_ref,
+    gate_ref,
+    up_ref,
+    down_ref,
+    out_ref,
+    acc,
+    rows_in,
+    resid,
+    pooled,
+    sums,
+    from_first,
+    from_second,
+    from_chain,
+    attn_send,
+    attn_recv,
+    chain_send,
+    chain_recv,
+    near_send,
+    near_recv,
+    far_send,
+    far_recv,
+    first_send,
+    first_recv,
+    second_send,
+    second_recv,
+    back_send,
+    back_recv,
+):
+    req = lax.axis_index("req")
+    z = lax.axis_index("mlp")
+    depth = lax.axis_size("mlp")
+    owned, _ = mine_ref.shape
+    half = owned // 2
+    group = 2 * depth * half
+    x_bit = (req // 2) % 2
+    y_bit = (req // 4) % 2
+    here = y_bit * 2 + x_bit
+    across_x = y_bit * 2 + 1 - x_bit
+    across_y = (1 - y_bit) * 2 + x_bit
+    across_both = (1 - y_bit) * 2 + 1 - x_bit
+    x_device = (req + 2 * (1 - 2 * x_bit), z)
+    y_device = (req + 4 * (1 - 2 * y_bit), z)
+    near = ((across_x, x_device), (across_y, y_device))
+    far = ((across_y, y_device), (across_x, x_device))
+    z_device = ((req, z + 1), (req, z - 1))
+    has_z = (z < depth - 1, z > 0)
+
+    barrier = pltpu.get_barrier_semaphore()
+    for device in (x_device, y_device):
+        pl.semaphore_signal(barrier, inc=1, device_id=device, device_id_type=MESH)
+    for way in range(2):
+
+        @pl.when(has_z[way])
+        def _():
+            pl.semaphore_signal(barrier, inc=1, device_id=z_device[way], device_id_type=MESH)
+
+    peers = 2 + has_z[0].astype(jnp.int32) + has_z[1].astype(jnp.int32)
+    pl.semaphore_wait(barrier, peers)
+
+    def remote(source, target, send, recv, device):
+        return pltpu.make_async_remote_copy(
+            src_ref=source,
+            dst_ref=target,
+            send_sem=send,
+            recv_sem=recv,
+            device_id=device,
+            device_id_type=MESH,
+        )
+
+    def block(which, h, j):
+        return pl.ds(pl.multiple_of(((which * 2 + h) * depth + j) * half, half), half)
+
+    def at_distance(step, body):
+        for way in range(2 if step else 1):
+            j = z + step if way == 0 else z - step
+            if step == 0:
+                body(j, way)
+            else:
+                inside = j < depth if way == 0 else j >= 0
+
+                @pl.when(inside)
+                def _():
+                    body(j, way)
+
+    def attn_copy(j, way):
+        return remote(
+            acc.at[j], rows_in.at[way, j], attn_send.at[way, j], attn_recv.at[way, j], z_device[way]
+        )
+
+    def own_part(j):
+        return partial_ref[pl.ds(pl.multiple_of(j * owned, owned), owned), :].astype(jnp.float32)
+
+    def attn_step(j, way):
+        upstream = has_z[1 - way]
+
+        @pl.when(upstream)
+        def _():
+            attn_copy(j, way).wait_recv()
+            acc[j] = (own_part(j) + rows_in[way, j].astype(jnp.float32)).astype(acc.dtype)
+
+        @pl.when(jnp.logical_not(upstream))
+        def _():
+            acc[j] = partial_ref[pl.ds(pl.multiple_of(j * owned, owned), owned), :]
+
+        attn_copy(j, way).start()
+
+    for step in range(depth - 1, 0, -1):
+        at_distance(step, attn_step)
+    resid[...] = mine_ref[...].astype(jnp.float32) + own_part(z)
+    for way in range(2):
+
+        @pl.when(has_z[1 - way])
+        def _():
+            attn_copy(z, way).wait_recv()
+            resid[...] += rows_in[way, z].astype(jnp.float32)
+
+    for h in range(2):
+        value = resid[pl.ds(h * half, half), :]
+        mean_sq = jnp.mean(value * value, axis=-1, keepdims=True)
+        normed = value * lax.rsqrt(mean_sq + norm_eps) * norm_ref[...]
+        pooled[block(here, h, z), :] = normed.astype(pooled.dtype)
+
+    def chain_copy(h, j, way):
+        rows = pooled.at[block(here, h, j), :]
+        return remote(rows, rows, chain_send.at[way, h, j], chain_recv.at[h, j], z_device[way])
+
+    def near_copy(h, j, arriving=False):
+        rows = pooled.at[block(near[h][0] if arriving else here, h, j), :]
+        return remote(rows, rows, near_send.at[h, j], near_recv.at[h, j], near[h][1])
+
+    def far_copy(h, k, j):
+        rows = pooled.at[block((here, near[h][0])[k], h, j), :]
+        return remote(rows, rows, far_send.at[h, k, j], far_recv.at[h, k, j], far[h][1])
+
+    def gather_step(step):
+        def body(j, way):
+            for h in range(2):
+                if step > 0:
+                    chain_copy(h, j, 1 - way).wait_recv()
+                for onward in range(2) if step == 0 else (1 - way,):
+
+                    @pl.when(has_z[onward])
+                    def _():
+                        chain_copy(h, j, onward).start()
+
+                near_copy(h, j).start()
+            for h in range(2):
+                far_copy(h, 0, j).start()
+
+        return body
+
+    def forward(j, way):
+        for h in range(2):
+            near_copy(h, j, True).wait_recv()
+            far_copy(h, 1, j).start()
+
+    for step in range(depth):
+        at_distance(step, gather_step(step))
+        if step > 0:
+            at_distance(step - 1, forward)
+    at_distance(depth - 1, forward)
+
+    def first_copy(h, k, j):
+        source = (far[h][0], across_both)[k]
+        return remote(
+            sums.at[block(source, h, j), :],
+            from_first.at[h, k, j],
+            first_send.at[h, k, j],
+            first_recv.at[h, k, j],
+            far[h][1],
+        )
+
+    def second_copy(h, j):
+        return remote(
+            sums.at[block(near[h][0], h, j), :],
+            from_second.at[h, j],
+            second_send.at[h, j],
+            second_recv.at[h, j],
+            near[h][1],
+        )
+
+    def back_copy(h, j, way):
+        return remote(
+            sums.at[block(here, h, j), :],
+            from_chain.at[way, h, j],
+            back_send.at[way, h, j],
+            back_recv.at[way, h, j],
+            z_device[way],
+        )
+
+    halves_in = ((), ((1, 0),), ((0, 0),), ((0, 1), (1, 1)))
+
+    def one_pack(i, carry):
+        x_of = (x_bit + i % 2) % 2
+        y_of = (y_bit + i // 2) % 2
+        which = y_of * 2 + x_of
+        for place in range(1, 4):
+
+            @pl.when(i == place)
+            def _():
+                for h, k in halves_in[place]:
+                    for j in range(depth):
+                        far_copy(h, k, j).wait_recv()
+
+        rows = pl.ds(pl.multiple_of(which * group, group), group)
+        value = pooled[rows, :]
+        dims = (((1,), (1,)), ((), ()))
+        gate = lax.dot_general(value, gate_ref[...], dims, preferred_element_type=jnp.float32)
+        upper = lax.dot_general(value, up_ref[...], dims, preferred_element_type=jnp.float32)
+        act = (gate / (1.0 + jnp.exp(-gate)) * upper).astype(jnp.bfloat16)
+        sums[rows, :] = jnp.dot(act, down_ref[...], preferred_element_type=jnp.float32).astype(
+            sums.dtype
+        )
+        for place in range(1, 4):
+
+            @pl.when(i == place)
+            def _():
+                for step in range(depth - 1, -1, -1):
+
+                    def body(j, way):
+                        for h, k in halves_in[place]:
+                            first_copy(h, k, j).start()
+
+                    at_distance(step, body)
+
+        return carry
+
+    lax.fori_loop(0, 4, one_pack, 0)
+
+    def second_step(j, way):
+        for h in range(2):
+            first_copy(h, 1, j).wait_recv()
+            rows = block(near[h][0], h, j)
+            total = sums[rows, :].astype(jnp.float32) + from_first[h, 1, j].astype(jnp.float32)
+            sums[rows, :] = total.astype(sums.dtype)
+            second_copy(h, j).start()
+
+    def all_here(h, j):
+        first_copy(h, 0, j).wait_recv()
+        second_copy(h, j).wait_recv()
+        return (
+            sums[block(here, h, j), :].astype(jnp.float32)
+            + from_first[h, 0, j].astype(jnp.float32)
+            + from_second[h, j].astype(jnp.float32)
+        )
+
+    def back_step(j, way):
+        for h in range(2):
+            rows = block(here, h, j)
+            total = all_here(h, j)
+            upstream = has_z[1 - way]
+
+            @pl.when(upstream)
+            def _():
+                back_copy(h, j, way).wait_recv()
+                sums[rows, :] = (total + from_chain[way, h, j].astype(jnp.float32)).astype(
+                    sums.dtype
+                )
+
+            @pl.when(jnp.logical_not(upstream))
+            def _():
+                sums[rows, :] = total.astype(sums.dtype)
+
+            back_copy(h, j, way).start()
+
+    for step in range(depth - 1, -1, -1):
+        at_distance(step, second_step)
+        if step < depth - 1:
+            at_distance(step + 1, back_step)
+    for h in range(2):
+        rows = pl.ds(h * half, half)
+        resid[rows, :] += all_here(h, z)
+        for way in range(2):
+
+            @pl.when(has_z[1 - way])
+            def _():
+                back_copy(h, z, way).wait_recv()
+                resid[rows, :] += from_chain[way, h, z].astype(jnp.float32)
+
+        out_ref[rows, :] = resid[rows, :].astype(out_ref.dtype)
+
+    def sent_step(step):
+        def body(j, way):
+            if step > 0:
+                attn_copy(j, way).wait_send()
+            for h in range(2):
+                for onward in range(2) if step == 0 else (1 - way,):
+
+                    @pl.when(has_z[onward])
+                    def _():
+                        chain_copy(h, j, onward).wait_send()
+
+                if step > 0:
+                    back_copy(h, j, way).wait_send()
+
+        return body
+
+    for step in range(depth):
+        at_distance(step, sent_step(step))
+    for h in range(2):
+        for j in range(depth):
+            near_copy(h, j).wait_send()
+            second_copy(h, j).wait_send()
+            for k in range(2):
+                far_copy(h, k, j).wait_send()
+                first_copy(h, k, j).wait_send()
+
+
+def exchange(partial, mine, norm, gate, up, down):
+    depth = lax.axis_size("mlp")
+    owned, width = mine.shape
+    half = owned // 2
+    pool = 4 * depth * owned
+    dma = pltpu.SemaphoreType.DMA
+    low = jnp.bfloat16
+    flops = 6 * pool * width * gate.shape[0]
+    return pl.pallas_call(
+        exchange_kernel,
+        out_shape=jax.ShapeDtypeStruct((owned, width), low),
+        in_specs=[pl.BlockSpec(memory_space=pltpu.VMEM)] * 6,
+        out_specs=pl.BlockSpec(memory_space=pltpu.VMEM),
+        scratch_shapes=[
+            pltpu.VMEM((depth, owned, width), low),
+            pltpu.VMEM((2, depth, owned, width), low),
+            pltpu.VMEM((owned, width), jnp.float32),
+            pltpu.VMEM((pool, width), low),
+            pltpu.VMEM((pool, width), low),
+            pltpu.VMEM((2, 2, depth, half, width), low),
+            pltpu.VMEM((2, depth, half, width), low),
+            pltpu.VMEM((2, 2, depth, half, width), low),
+            dma((2, depth)),
+            dma((2, depth)),
+            dma((2, 2, depth)),
+            dma((2, depth)),
+            dma((2, depth)),
+            dma((2, depth)),
+            dma((2, 2, depth)),
+            dma((2, 2, depth)),
+            dma((2, 2, depth)),
+            dma((2, 2, depth)),
+            dma((2, depth)),
+            dma((2, depth)),
+            dma((2, 2, depth)),
+            dma((2, 2, depth)),
+        ],
+        cost_estimate=pl.CostEstimate(
+            flops=flops, bytes_accessed=6 * gate.shape[0] * width, transcendentals=0
+        ),
+        compiler_params=pltpu.CompilerParams(
+            collective_id=0, has_side_effects=True, vmem_limit_bytes=52 * 1024 * 1024
+        ),
+    )(partial, mine, norm.reshape(1, width), gate, up, down)
 
 
 def per_device(
@@ -91,44 +444,13 @@
     probs = (weights / jnp.sum(weights, axis=-1, keepdims=True)).astype(jnp.bfloat16)
     context = jnp.einsum("kgst,tkd->skgd", probs, value, preferred_element_type=jnp.float32)
     context = context.astype(jnp.bfloat16).reshape(slots, local_kv * group_q * head_dim)
-    attn_out = lax.psum_scatter(
-        jnp.dot(context, o_weight, preferred_element_type=jnp.float32),
-        "mlp",
-        scatter_dimension=0,
-        tiled=True,
-    )
-    mine = lax.dynamic_slice_in_dim(tokens, lax.axis_index("mlp") * owned, owned, 0).astype(
-        jnp.float32
-    )
-    resid = mine + attn_out
-    mlp_in = rms_scale(resid, mlp_norm).astype(jnp.bfloat16)
+    partial = jnp.dot(context, o_weight, preferred_element_type=jnp.float32).astype(jnp.bfloat16)
+    mine = lax.dynamic_slice_in_dim(tokens, lax.axis_index("mlp") * owned, owned, 0)
     req_bits = lax.axis_size("req").bit_length() - 1
-    low_bits = 2
-    req_index = lax.axis_index("req")
-    pooled = lax.all_gather(mlp_in, "mlp", axis=0, tiled=True)
-    for bit in range(low_bits):
-        partner = from_partner(pooled, "req", bit)
-        upper_side = req_index // 2**bit % 2 == 1
-        lower_rows = jnp.where(upper_side, partner, pooled)
-        upper_rows = jnp.where(upper_side, pooled, partner)
-        pooled = jnp.concatenate([lower_rows, upper_rows], axis=0)
-    units = jnp.concatenate([gate_up, down_weight[:, None, :]], axis=1)
-    for bit in range(low_bits, req_bits):
-        far_units = from_partner(units, "req", bit)
-        units = jnp.concatenate([units, far_units], axis=0)
-    partial_out = feed_forward(pooled, units[:, 0:2, :], units[:, 2, :])
-    for bit in reversed(range(low_bits)):
-        half_rows = partial_out.shape[0] // 2
-        upper_side = req_index // 2**bit % 2 == 1
-        lower_part = partial_out[:half_rows]
-        upper_part = partial_out[half_rows:]
-        kept = jnp.where(upper_side, upper_part, lower_part)
-        sent = jnp.where(upper_side, lower_part, upper_part)
-        partial_out = kept + from_partner(sent.astype(jnp.bfloat16), "req", bit).astype(sent.dtype)
-    mlp_out = lax.psum_scatter(
-        partial_out.astype(jnp.bfloat16), "mlp", scatter_dimension=0, tiled=True
-    ).astype(jnp.float32)
-    layer_out = (resid + mlp_out).astype(jnp.bfloat16)
+    units = [gate_up[:, 0, :], gate_up[:, 1, :], down_weight]
+    for bit in (0, *range(3, req_bits)):
+        units = [jnp.concatenate([part, from_partner(part, "req", bit)], axis=0) for part in units]
+    layer_out = exchange(partial, mine, mlp_norm, *units)
     return (layer_out, kv_cache)
 
 

time: 335 us -> 183 us (0.55)
  waiting for transfers between devices: 238 us -> 0.01 us
  Pallas kernels: 0 us -> 133 us
  matrix products: 30.4 us -> 7.79 us
  other arithmetic: 37.4 us -> 18.9 us
  between operations: 14.1 us -> 0.93 us
  local copies, waits for them, and re-layouts: 10.2 us -> 20.7 us
  starting transfers between devices: 4.84 us -> 1.17 us
    pallas_call x0 -> x1, Pallas kernels: none -> 133 us  [exchange(): pl.pallas_call(exchange_kernel, out_shape=jax.ShapeDtypeStruct((owned, wi...]
    ppermute x5 -> x3, waiting for transfers between devices: 129 us -> 0.01 us  [from_partner(): return lax.ppermute(value, axis, pairs)]
    reduce_scatter x2 -> x0, waiting for transfers between devices: 83 us -> none  [the longest x1 54.9 us: per_device(): lax.psum_scatter(jnp.dot(context, o_weight, preferred_element_type=jnp.fl...]
    all_gather x1 -> x0, waiting for transfers between devices: 25.9 us -> none  [per_device(): pooled = lax.all_gather(mlp_in, 'mlp', axis=0, tiled=True)]
    dot_general x2 -> x0, matrix products: 18.8 us -> none  [the longest x1 13.9 us: feed_forward(): return jnp.dot(act, unit_down, preferred_element_type=jnp.float32)]
    convert_element_type x5 -> x0, other arithmetic: 10.3 us -> none  [the longest x2 4.74 us: per_device(): sent.astype(jnp.bfloat16)]
    slice x0 -> x1, local copies, waits for them, and re-layouts: none -> 8 us  [per_device(): units = [gate_up[:, 0, :], gate_up[:, 1, :], down_weight]]
    select_n x2 -> x0, other arithmetic: 6.07 us -> none  [per_device(): lower_rows = jnp.where(upper_side, partner, pooled)]
  transfers between devices with their start and end apart: 8 -> 3, of which waited for: 7 -> 0; matrix products, arithmetic and copies ran while one was open for 5% -> 22% of each run, Pallas kernels for 0% -> 0%
where the time goes in v1:
time: 183 us; the launch traced here: 182 us
  Pallas kernels  133 us (73%)
  local copies, waits for them, and re-layouts  20.7 us (11%)
  other arithmetic  18.9 us (10%)
  matrix products  7.79 us (4%)
    pallas_call x1, Pallas kernels, exchange(): pl.pallas_call(exchange_kernel, out_shape=jax.ShapeDtypeStruct((owned, wi...  133 us
    concatenate x3, other arithmetic, per_device(): jnp.concatenate([part, from_partner(part, 'req', bit)], axis=0)  9.83 us
    slice x1, local copies, waits for them, and re-layouts, per_device(): units = [gate_up[:, 0, :], gate_up[:, 1, :], down_weight]  8 us
    unnamed x34, local copies, waits for them, and re-layouts  5.24 us
  transfers between devices with their start and end apart: 3, of which 0 were waited for; matrix products, arithmetic and copies ran while one was open for 22% of the time, Pallas kernels for 0%

profile of v1, /device:TPU:0, one launch (start us, length us, event | category | flops | bytes accessed | tf_op | source)
XLA Modules:
  0.0 182.1 jit_solution(8887661450944998603)
XLA Ops:
  1.1 8.0 %fusion.24 = (bf16[304,1,2560]{2,1,0:T(2,128)(2,1)S(1)}, bf16[304,1,2560]{2,1,0:T(2,128)(2,1)S(1)}) fusion(bf16[304,2,2560]{2,1,0:T(2,128)(2,1)} %param.20), kind=kLoop, calls=%fused_computation.61 | loop fusion | bytes 6225920 | tf_op jit(solution)/shard_map/slice | solution.py:450
  10.3 0.6 copy-done
  11.2 1.6 copy-done.10
  12.8 2.3 %fusion = f32[256,2,768]{2,0,1:T(8,128)S(1)} fusion(bf16[2560,2,768]{2,1,0:T(2,128)(2,1)S(1)} %copy-done.10, bf16[256,2560]{1,0:T(8,128)(2,1)S(1)} %copy-done, f32[2560]{0:T(1024)S(1)} %copy-done.11, f32[256]{0:T(256)S(1)} %add_rsqrt_fusion.2), kind=kOutput, calls=%fused_computation.1 | convolution fusion | flops 2015887360 | bytes 10759168 | tf_op jit(solution)/shard_map/sd,dkc->skc/dot_general | solution.py:428
  15.3 1.0 copy-done.1
  16.2 1.6 fusion.25
  18.1 0.7 fusion.16
  18.9 2.6 %reshape.240 = f32[256,2,4,128]{3,2,0,1:T(4,128)} reshape(f32[256,2,512]{2,0,1:T(8,128)} %get-tuple-element.14) | data formatting | bytes 2097152 | tf_op jit(solution)/shard_map/reshape | solution.py:429
  21.4 1.9 %multiply_reduce_fusion = f32[256,2,4]{2,0,1:T(8,128)S(1)} fusion(f32[256,2,4,128]{3,2,0,1:T(4,128)} %reshape.240), kind=kLoop, calls=%fused_computation.25 | loop fusion | flops 522240 | bytes 1056768 | tf_op jit(solution)/shard_map/reduce_sum | solution.py:22
  24.0 1.1 multiply_multiply_fusion
  25.2 1.6 fusion.10
  26.9 1.4 subtract_convert_fusion
  28.3 0.8 copy_bitcast_fusion.2
  29.2 2.2 %scatter_fusion = bf16[2,16,16,2,128]{4,2,3,1,0:T(8,128)(2,1)S(1)} fusion(bf16[2,16,16,2,128]{4,2,3,1,0:T(8,128)(2,1)S(1)} %broadcast_in_dim.10, s32[16]{0:T(128)S(1)} %fusion.20, bf16[16,2,16,2,128]{4,2,3,1,0:T(8,128)(2,1)} %copy_bitcast_fusion.2), kind=kCustom, calls=%fused_computation | custom fusion | bytes 786496 | tf_op jit(solution)/shard_map/scatter | solution.py:438
  31.4 0.9 copy.55
  32.3 2.3 %fusion.5 = (f32[2,4,256]{2,1,0:T(4,128)S(1)}, f32[2,256,256,4]{2,1,3,0:T(8,128)S(1)}) fusion(pred[256,256]{0,1:T(8,128)(4,1)} %fusion.16, bf16[256,2,4,64]{3,0,2,1:T(8,128)(2,1)} %get-tuple-element.17, bf16[256,2,4,64]{3,0,2,1:T(8,128)(2,1)} %get-tuple-element.16, bf16[256,2,64]{2,0,1:T(8,128)(2,1)} %copy-done.4, bf16[256,2,64]{2,0,1:T(8,128)(2,1)} %copy-done.3), kind=kOutput, calls=%fused_computation.14 | convolution fusion | flops 137099264 | bytes 2826240 | tf_op jit(solution)/shard_map/skgd,tkd->kgst/dot_general | solution.py:439
  34.6 1.7 convolution_convert_fusion.1
  36.3 1.0 constant_dynamic-slice_fusion.mine_ref
  37.4 1.5 convolution_convert_fusion.partial_ref
  38.9 3.2 %pad_maximum_fusion.2.down_ref = bf16[608,2560]{1,0:T(8,128)(2,1)} fusion(bf16[304,2560]{1,0:T(8,128)(2,1)} %collective-permute-done.2, bf16[304,2560]{1,0:T(8,128)(2,1)S(1)} %copy-done.2), kind=kLoop, calls=%fused_computation.8 | loop fusion | flops 6225920 | bytes 6225920 | tf_op jit(solution)/shard_map/concatenate | solution.py:452
  42.2 3.3 %pad_maximum_fusion.gate_ref = bf16[608,2560]{1,0:T(8,128)(2,1)} fusion(bf16[304,2560]{1,0:T(8,128)(2,1)} %collective-permute-done, bf16[304,2560]{1,0:T(8,128)(2,1)S(1)} %bitcast.55), kind=kLoop, calls=%fused_computation.6 | loop fusion | flops 6225920 | bytes 6225920 | tf_op jit(solution)/shard_map/concatenate | solution.py:452
  45.5 3.3 %pad_maximum_fusion.1.up_ref = bf16[608,2560]{1,0:T(8,128)(2,1)} fusion(bf16[304,2560]{1,0:T(8,128)(2,1)} %collective-permute-done.1, bf16[304,2560]{1,0:T(8,128)(2,1)S(1)} %bitcast.57), kind=kLoop, calls=%fused_computation.7 | loop fusion | flops 6225920 | bytes 6225920 | tf_op jit(solution)/shard_map/concatenate | solution.py:452
  48.8 132.6 %shard_map.122 = bf16[64,2560]{1,0:T(8,128)(2,1)S(1)} custom-call(bf16[256,2560]{1,0:T(8,128)(2,1)S(1)} %convolution_convert_fusion.partial_ref, bf16[64,2560]{1,0:T(8,128)(2,1)S(1)} %constant_dynamic-slice_fusion.mine_ref, f32[1,2560]{1,0:T(1,128)S(1)} %reshape.242.norm_ref, bf16[608,2560]{1,0:T(8,128)(2,1)} %pad_maximum_fusion.gate_ref, ...), custom_call_target="tpu_custom_call" | custom-call | flops 9563013120 | bytes 9338880 | tf_op jit(solution)/shard_map/pallas_call | solution.py:368
  181.3 0.7 copy.76
  (52 shorter events, 3.3 us)
Async XLA Ops:
  0.6 38.3 %collective-permute-start.2 = (bf16[304,2560]{1,0:T(8,128)(2,1)}, bf16[304,2560]{1,0:T(8,128)(2,1)}, u32[]{:S(2)}, u32[]{:S(2)}) collective-permute-start(bf16[304,2560]{1,0:T(8,128)(2,1)} %param.21), channel_id=1, source_target_pairs={{0,4},{4,0},{8,12},{12,8},{16,20},{20,16},{24,28},{28,24},{1,5},{5... | collective-permute-start | bytes 4669448 | tf_op jit(solution)/shard_map/ppermute | solution.py:18
  9.2 3.6 %copy-start.10 = (bf16[2560,2,768]{2,1,0:T(2,128)(2,1)S(1)}, bf16[2560,2,768]{2,1,0:T(2,128)(2,1)}, u32[]{:S(2)}) copy-start(bf16[2560,2,768]{2,1,0:T(2,128)(2,1)} %param.15) | copy-start | bytes 23592964
  9.4 1.5 copy-start
  9.4 32.8 %collective-permute-start = (bf16[304,2560]{1,0:T(8,128)(2,1)S(1)}, bf16[304,2560]{1,0:T(8,128)(2,1)}, u32[]{:S(2)}, u32[]{:S(2)}) collective-permute-start(bf16[304,2560]{1,0:T(8,128)(2,1)S(1)} %bitcast.54), channel_id=1, source_target_pairs={{0,4},{4,0},{8,12},{12,8},{16,20},{20,16},{24,28},{28,24},{1,5},{5... | collective-permute-start | bytes 4669448 | tf_op jit(solution)/shard_map/ppermute | solution.py:18
  9.5 3.3 %copy-start.11 = (f32[2560]{0:T(1024)S(1)}, f32[2560]{0:T(1024)}, u32[]{:S(2)}) copy-start(f32[2560]{0:T(1024)} %param.14) | copy-start | bytes 30724
  9.7 35.7 %collective-permute-start.1 = (bf16[304,2560]{1,0:T(8,128)(2,1)S(1)}, bf16[304,2560]{1,0:T(8,128)(2,1)}, u32[]{:S(2)}, u32[]{:S(2)}) collective-permute-start(bf16[304,2560]{1,0:T(8,128)(2,1)S(1)} %bitcast.56), channel_id=1, source_target_pairs={{0,4},{4,0},{8,12},{12,8},{16,20},{20,16},{24,28},{28,24},{1,5},{5... | collective-permute-start | bytes 4669448 | tf_op jit(solution)/shard_map/ppermute | solution.py:18
  15.1 1.2 copy-start.1
  15.1 2.7 %copy-start.12 = (s32[1,16]{1,0:T(1,128)S(1)}, s32[1,16]{1,0:T(1,128)}, u32[]{:S(2)}) copy-start(s32[1,16]{1,0:T(1,128)} %param.13) | copy-start | bytes 196
  15.1 2.7 %copy-start.9 = (s32[1,4]{1,0:T(1,128)S(1)}, s32[1,4]{1,0:T(1,128)}, u32[]{:S(2)}) copy-start(s32[1,4]{1,0:T(1,128)} %param.12) | copy-start | bytes 52
  17.8 6.1 %copy-start.7 = (f32[128]{0:T(128)S(1)}, f32[128]{0:T(128)}, u32[]{:S(2)}) copy-start(f32[128]{0:T(128)} %param.17) | copy-start | bytes 1540
  18.9 6.4 %copy-start.8 = (f32[128]{0:T(128)S(1)}, f32[128]{0:T(128)}, u32[]{:S(2)}) copy-start(f32[128]{0:T(128)} %param.16) | copy-start | bytes 1540
  25.2 3.1 %copy-start.3 = (bf16[256,2,64]{2,0,1:T(8,128)(2,1)}, bf16[256,2,64]{2,0,1:T(8,128)(2,1)S(1)}, u32[]{:S(2)}) copy-start(bf16[256,2,64]{2,0,1:T(8,128)(2,1)S(1)} %get-tuple-element.18) | copy-start | bytes 196612
  25.2 3.1 %copy-start.4 = (bf16[256,2,64]{2,0,1:T(8,128)(2,1)}, bf16[256,2,64]{2,0,1:T(8,128)(2,1)S(1)}, u32[]{:S(2)}) copy-start(bf16[256,2,64]{2,0,1:T(8,128)(2,1)S(1)} %get-tuple-element.19) | copy-start | bytes 196612
  25.2 3.9 %copy-start.6 = (f32[2560]{0:T(1024)S(1)}, f32[2560]{0:T(1024)}, u32[]{:S(2)}) copy-start(f32[2560]{0:T(1024)} %param.19) | copy-start | bytes 30724
  29.1 5.5 %copy-start.5 = (pred[256,256]{0,1:T(8,128)(4,1)S(1)}, pred[256,256]{0,1:T(8,128)(4,1)}, u32[]{:S(2)}) copy-start(pred[256,256]{0,1:T(8,128)(4,1)} %fusion.16) | copy-start | bytes 196612
  32.3 5.0 %slice-start = ((s8[5242880]{0:T(1024)(128)(4,1)}), s8[4194304]{0:T(1024)(128)(4,1)S(1)}, s32[]{:S(2)}) async-start(s8[5242880]{0:T(1024)(128)(4,1)} %bitcast.64), calls=%async_computation | async-start | bytes 8388608
  34.6 2.7 %slice-start.1 = ((s8[5242880]{0:T(1024)(128)(4,1)}), s8[1048576]{0:T(1024)(128)(4,1)S(1)}, s32[]{:S(2)}) async-start(s8[5242880]{0:T(1024)(128)(4,1)} %bitcast.64), calls=%async_computation.1 | async-start | bytes 2097152
  37.3 1.6 copy-start.2

commit v2 on v1

--- a/solution.py
+++ b/solution.py
@@ -50,10 +50,14 @@
     partial_ref,
     mine_ref,
     norm_ref,
+    pairs_ref,
+    far_pairs_ref,
+    down_own_ref,
+    far_down_ref,
+    out_ref,
     gate_ref,
     up_ref,
     down_ref,
-    out_ref,
     acc,
     rows_in,
     resid,
@@ -76,6 +80,7 @@
     second_recv,
     back_send,
     back_recv,
+    unit_sem,
 ):
     req = lax.axis_index("req")
     z = lax.axis_index("mlp")
@@ -108,6 +113,21 @@
     peers = 2 + has_z[0].astype(jnp.int32) + has_z[1].astype(jnp.int32)
     pl.semaphore_wait(barrier, peers)
 
+    count = down_own_ref.shape[0]
+    unit_copies = []
+    for side, (pairs, down) in enumerate(
+        ((pairs_ref, down_own_ref), (far_pairs_ref, far_down_ref))
+    ):
+        place = pl.ds(side * count, count)
+        for k, (source, target) in enumerate(
+            ((pairs.at[0], gate_ref), (pairs.at[1], up_ref), (down, down_ref))
+        ):
+            unit_copies.append(
+                pltpu.make_async_copy(source, target.at[place, :], unit_sem.at[side, k])
+            )
+    for copy in unit_copies:
+        copy.start()
+
     def remote(source, target, send, recv, device):
         return pltpu.make_async_remote_copy(
             src_ref=source,
@@ -276,6 +296,8 @@
 
         return carry
 
+    for copy in unit_copies:
+        copy.wait()
     lax.fori_loop(0, 4, one_pack, 0)
 
     def second_step(j, way):
@@ -357,20 +379,25 @@
                 first_copy(h, k, j).wait_send()
 
 
-def exchange(partial, mine, norm, gate, up, down):
+def exchange(partial, mine, norm, pairs, far_pairs, down, far_down):
     depth = lax.axis_size("mlp")
     owned, width = mine.shape
     half = owned // 2
     pool = 4 * depth * owned
     dma = pltpu.SemaphoreType.DMA
     low = jnp.bfloat16
-    flops = 6 * pool * width * gate.shape[0]
+    units = 2 * down.shape[0]
+    flops = 6 * pool * width * units
     return pl.pallas_call(
         exchange_kernel,
         out_shape=jax.ShapeDtypeStruct((owned, width), low),
-        in_specs=[pl.BlockSpec(memory_space=pltpu.VMEM)] * 6,
+        in_specs=[pl.BlockSpec(memory_space=pltpu.VMEM)] * 3
+        + [pl.BlockSpec(memory_space=pl.ANY)] * 4,
         out_specs=pl.BlockSpec(memory_space=pltpu.VMEM),
         scratch_shapes=[
+            pltpu.VMEM((units, width), low),
+            pltpu.VMEM((units, width), low),
+            pltpu.VMEM((units, width), low),
             pltpu.VMEM((depth, owned, width), low),
             pltpu.VMEM((2, depth, owned, width), low),
             pltpu.VMEM((owned, width), jnp.float32),
@@ -393,14 +420,15 @@
             dma((2, depth)),
             dma((2, 2, depth)),
             dma((2, 2, depth)),
+            dma((2, 3)),
         ],
         cost_estimate=pl.CostEstimate(
-            flops=flops, bytes_accessed=6 * gate.shape[0] * width, transcendentals=0
+            flops=flops, bytes_accessed=6 * units * width, transcendentals=0
         ),
         compiler_params=pltpu.CompilerParams(
             collective_id=0, has_side_effects=True, vmem_limit_bytes=52 * 1024 * 1024
         ),
-    )(partial, mine, norm.reshape(1, width), gate, up, down)
+    )(partial, mine, norm.reshape(1, width), pairs, far_pairs, down, far_down)
 
 
 def per_device(
@@ -447,10 +475,14 @@
     partial = jnp.dot(context, o_weight, preferred_element_type=jnp.float32).astype(jnp.bfloat16)
     mine = lax.dynamic_slice_in_dim(tokens, lax.axis_index("mlp") * owned, owned, 0)
     req_bits = lax.axis_size("req").bit_length() - 1
-    units = [gate_up[:, 0, :], gate_up[:, 1, :], down_weight]
-    for bit in (0, *range(3, req_bits)):
-        units = [jnp.concatenate([part, from_partner(part, "req", bit)], axis=0) for part in units]
-    layer_out = exchange(partial, mine, mlp_norm, *units)
+    pairs = lax.optimization_barrier(jnp.transpose(gate_up, (1, 0, 2)))
+    down = down_weight
+    for bit in range(3, req_bits):
+        pairs = jnp.concatenate([pairs, from_partner(pairs, "req", bit)], axis=1)
+        down = jnp.concatenate([down, from_partner(down, "req", bit)], axis=0)
+    far_pairs = from_partner(pairs, "req", 0)
+    far_down = from_partner(down, "req", 0)
+    layer_out = exchange(partial, mine, mlp_norm, pairs, far_pairs, down, far_down)
     return (layer_out, kv_cache)
 
 

time: 183 us -> 151 us (0.83)
  other arithmetic: 18.9 us -> 4.18 us
  local copies, waits for them, and re-layouts: 20.7 us -> 10.1 us
  Pallas kernels: 133 us -> 126 us
    concatenate x3 -> x0, other arithmetic: 9.83 us -> none  [per_device(): jnp.concatenate([part, from_partner(part, 'req', bit)], axis=0)]
    slice x1 -> x0, local copies, waits for them, and re-layouts: 8 us -> none  [per_device(): units = [gate_up[:, 0, :], gate_up[:, 1, :], down_weight]]
    pallas_call x1, Pallas kernels: 133 us -> 126 us  [exchange(): pl.pallas_call(exchange_kernel, out_shape=jax.ShapeDtypeStruct((owned, wi...]
    dot_general x1, matrix products: 2.26 us -> 5.49 us  [per_device(): jnp.einsum('sd,dkc->skc', normed, qkv_weight, preferred_element_type=jnp....]
    reshape x1, local copies, waits for them, and re-layouts: 2.55 us -> 0.36 us  [per_device(): qkv[:, :, :group_q * head_dim].reshape(slots, local_kv, group_q, head_dim)]
    unnamed x34 -> x23, local copies, waits for them, and re-layouts: 5.24 us -> 6.6 us
  transfers between devices with their start and end apart: 3 -> 2, of which waited for: 0 -> 0; matrix products, arithmetic and copies ran while one was open for 22% -> 15% of each run, Pallas kernels for 0% -> 0%
where the time goes in v2:
time: 151 us
  Pallas kernels  126 us (83%)
  local copies, waits for them, and re-layouts  10.1 us (7%)
  matrix products  9.57 us (6%)
  other arithmetic  4.18 us (3%)
    pallas_call x1, Pallas kernels, exchange(): pl.pallas_call(exchange_kernel, out_shape=jax.ShapeDtypeStruct((owned, wi...  126 us
    unnamed x23, local copies, waits for them, and re-layouts  6.6 us
    dot_general x1, matrix products, per_device(): jnp.einsum('sd,dkc->skc', normed, qkv_weight, preferred_element_type=jnp....  5.49 us
  transfers between devices with their start and end apart: 2, of which 0 were waited for; matrix products, arithmetic and copies ran while one was open for 15% of the time, Pallas kernels for 0%

profile of v2, /device:TPU:0, one launch (start us, length us, event | category | flops | bytes accessed | tf_op | source)
XLA Modules:
  0.0 151.1 jit_solution(12513151691005215186)
XLA Ops:
  0.7 0.5 collective-permute-start.1
  1.2 3.8 %copy.65 = bf16[304,2,2560]{2,0,1:T(8,128)(2,1)} copy(bf16[304,2,2560]{2,1,0:T(2,128)(2,1)} %param.20) | data formatting | bytes 6225920 | tf_op args[9]
  5.0 0.1 collective-permute-start
  5.2 0.3 fusion.2
  5.5 5.5 %fusion = f32[256,2,768]{2,0,1:T(8,128)S(1)} fusion(bf16[2560,2,768]{2,1,0:T(2,128)(2,1)} %param.15, bf16[256,2560]{1,0:T(8,128)(2,1)S(1)} %copy-done, f32[2560]{0:T(1024)S(1)} %copy-done.6, f32[256]{0:T(256)S(1)} %add_rsqrt_fusion.2), kind=kOutput, calls=%fused_computation.1 | convolution fusion | flops 2015887360 | bytes 10759168 | tf_op jit(solution)/shard_map/sd,dkc->skc/dot_general | solution.py:456
  11.1 0.1 multiply_reduce_fusion.1
  11.2 0.9 copy-done.1
  12.2 0.3 fusion.24
  12.5 0.2 reduce-window.8
  12.9 0.4 reshape.240
  13.3 0.6 multiply_reduce_fusion
  14.0 0.5 multiply_cosine_fusion
  14.6 1.1 multiply_multiply_fusion
  15.7 0.2 subtract_convert_fusion.1
  15.8 0.3 fusion.10
  16.2 0.5 subtract_convert_fusion
  16.9 1.3 scatter_fusion
  18.2 0.9 copy.51
  19.1 0.9 fusion.5
  20.0 1.4 constant_dynamic-slice_fusion.mine_ref
  21.4 1.7 %convolution_convert_fusion.1 = bf16[2,128,4,256]{3,1,2,0:T(8,128)(2,1)S(1)} fusion(f32[2,256,256,4]{2,1,3,0:T(8,128)S(1)} %get-tuple-element.21, f32[2,4,256]{2,1,0:T(4,128)S(1)} %get-tuple-element.20, pred[256,256]{0,1:T(8,128)(4,1)S(1)} %fusion.16, f32[256,2,768]{2,0,1:T(8,128)} %copy-done.1), kind=kOutput, calls=%fused_computation.16 | convolution fusion | flops 136577024 | bytes 2826240 | tf_op jit(solution)/shard_map/kgst,tkd->skgd/dot_general | solution.py:473
  23.1 1.5 %convolution_convert_fusion.partial_ref = bf16[256,2560]{1,0:T(8,128)(2,1)S(1)} fusion(bf16[256,1024]{0,1:T(8,128)(2,1)S(1)} %bitcast.59, bf16[1024,2560]{1,0:T(8,128)(2,1)S(1)} %bitcast.58), kind=kOutput, calls=%fused_computation.3 | convolution fusion | flops 1342832640 | bytes 7077888 | tf_op jit(solution)/shard_map/dot_general | solution.py:475
  24.7 125.6 %shard_map.122 = bf16[64,2560]{1,0:T(8,128)(2,1)S(1)} custom-call(bf16[256,2560]{1,0:T(8,128)(2,1)S(1)} %convolution_convert_fusion.partial_ref, bf16[64,2560]{1,0:T(8,128)(2,1)S(1)} %constant_dynamic-slice_fusion.mine_ref, f32[1,2560]{1,0:T(1,128)S(1)} %reshape.242.norm_ref, bf16[2,304,2560]{2,1,0:T(8,128)(2,1)} %bitcast.49.pairs_ref, ...), custom_call_target="tpu_custom_call" | custom-call | flops 9563013120 | bytes 9338880 | tf_op jit(solution)/shard_map/pallas_call | solution.py:391
  150.3 0.7 copy.68
  (35 shorter events, 0.7 us)
Async XLA Ops:
  0.6 4.5 %copy-start = (bf16[256,2560]{1,0:T(8,128)(2,1)S(1)}, bf16[256,2560]{1,0:T(8,128)(2,1)}, u32[]{:S(2)}) copy-start(bf16[256,2560]{1,0:T(8,128)(2,1)} %param.11) | copy-start | bytes 3932164
  0.6 4.9 %copy-start.6 = (f32[2560]{0:T(1024)S(1)}, f32[2560]{0:T(1024)}, u32[]{:S(2)}) copy-start(f32[2560]{0:T(1024)} %param.14) | copy-start | bytes 30724
  0.7 24.0 %collective-permute-start.1 = (bf16[304,2560]{1,0:T(8,128)(2,1)}, bf16[304,2560]{1,0:T(8,128)(2,1)}, u32[]{:S(2)}, u32[]{:S(2)}) collective-permute-start(bf16[304,2560]{1,0:T(8,128)(2,1)} %down_own_ref.1), channel_id=1, source_target_pairs={{0,4},{4,0},{8,12},{12,8},{16,20},{20,16},{24,28},{28,24},{1,5},{5... | collective-permute-start | bytes 4669448 | tf_op jit(solution)/shard_map/ppermute | solution.py:18
  5.0 19.7 %collective-permute-start = (bf16[2,304,2560]{2,1,0:T(8,128)(2,1)}, bf16[2,304,2560]{2,1,0:T(8,128)(2,1)}, u32[]{:S(2)}, u32[]{:S(2)}) collective-permute-start(bf16[2,304,2560]{2,1,0:T(8,128)(2,1)} %bitcast.49.pairs_ref), channel_id=1, source_target_pairs={{0,4},{4,0},{8,12},{12,8},{16,20},{20,16},{24,28},{28,24},{1,5},{5... | collective-permute-start | bytes 9338888 | tf_op jit(solution)/shard_map/ppermute | solution.py:18
  11.0 1.1 copy-start.1
  11.0 1.4 copy-start.5
  12.4 1.6 %copy-start.7 = (s32[1,16]{1,0:T(1,128)S(1)}, s32[1,16]{1,0:T(1,128)}, u32[]{:S(2)}) copy-start(s32[1,16]{1,0:T(1,128)} %param.13) | copy-start | bytes 196
  12.5 2.1 %copy-start.3 = (f32[128]{0:T(128)S(1)}, f32[128]{0:T(128)}, u32[]{:S(2)}) copy-start(f32[128]{0:T(128)} %param.17) | copy-start | bytes 1540
  13.3 2.6 %copy-start.4 = (f32[128]{0:T(128)S(1)}, f32[128]{0:T(128)}, u32[]{:S(2)}) copy-start(f32[128]{0:T(128)} %param.16) | copy-start | bytes 1540
  16.2 0.7 copy-start.2
  19.1 4.0 %slice-start = ((s8[5242880]{0:T(1024)(128)(4,1)}), s8[4194304]{0:T(1024)(128)(4,1)S(1)}, s32[]{:S(2)}) async-start(s8[5242880]{0:T(1024)(128)(4,1)} %bitcast.57), calls=%async_computation | async-start | bytes 8388608
  21.4 1.7 %slice-start.1 = ((s8[5242880]{0:T(1024)(128)(4,1)}), s8[1048576]{0:T(1024)(128)(4,1)S(1)}, s32[]{:S(2)}) async-start(s8[5242880]{0:T(1024)(128)(4,1)} %bitcast.57), calls=%async_computation.1 | async-start | bytes 2097152
